TPU v7x, 1024 devices: a whole 8x8x8 slice. The times are simulated.
1024 devices in a mesh: dom: 64 (over y, x), group: 16 (over z, core).
Axes of the slice: x: 8, y: 8, z: 8, core: 2. Of those that a mesh axis runs over, the one named last changes fastest.
Arguments:
- features: bfloat16 [16, 64, 512, 256], P('group', 'dom'), may hold values from -6 to 6
- new_owner: int32 [16, 64, 64, 1], P('group', 'dom'), may hold values from 0 to 63; in each aligned block of 64 rows (0 to 63, 64 to 127, ..., all dimensions but the last counted through in order) at most 2 rows name the same one
- rim_rows: int32 [16, 64, 4, 128], P('group', 'dom'), may hold values from 0 to 1023
- rim_counts: int32 [16, 64, 4], P('group', 'dom'), may hold values from 1 to 128, 256 in all within a row
- tile_sources: int32 [16, 64, 8, 4], P('group', 'dom'), may hold values from 0 to 11
- tile_values: bfloat16 [16, 64, 8, 4, 128, 128], P('group', 'dom'), may hold values from -0.25 to 0.25
- w_self: bfloat16 [256, 256], replicated, may hold values from -0.375 to 0.375
- w_neigh: bfloat16 [256, 256], replicated, may hold values from -0.375 to 0.375
- cotangent: bfloat16 [16, 64, 1024, 256], P('group', 'dom'), may hold values from -6 to 6
Outputs:
- layer_out: bfloat16 [16, 64, 1024, 256], P('group', 'dom')
- grad_self: float32 [256, 256], replicated
- grad_neigh: float32 [256, 256], replicated
Inputs may be any that keep to these rules, and one draw needn't show every extreme that they name: `new_owner`: no device sends more than 2 blocks to one new owner; some device sends exactly 2 to one. `rim_rows`: slot p of device (g, d) goes to: p = 0 the next device along dom, p = 1 the previous along dom, p = 2 the next along group, p = 3 the previous along group. `rim_counts`: some peer of every device gets exactly 128 rows. `tile_sources`: tiles below 8 are the device's own; tile 8 holds slot 0 of the previous device along dom, tile 8 + 1 slot 1 of the next along dom, tile 8 + 2 slot 2 of the previous along group, tile 8 + 3 slot 3 of the next along group.
All inputs are finite; a program needn't handle non-finite values.
Results may differ from a plain program's by a relative error of at most 0.0061.
Values may be sent and summed in bfloat16 or wider, within the bound.
A program may use at most 32 MiB of HBM per device.

v0:
```python
import jax
import jax.numpy as jnp
from jax import lax
from jax.sharding import PartitionSpec as P


def padded(block, sides, width):
    for axis, dim in sides:
        count = lax.axis_size(axis)
        forward = [(i, i + 1) for i in range(count - 1)]
        forward.append((count - 1, 0))
        backward = [(target, source) for source, target in forward]
        low = lax.ppermute(
            lax.slice_in_dim(block, block.shape[dim] - width, None, axis=dim), axis, forward
        )
        high = lax.ppermute(lax.slice_in_dim(block, 0, width, axis=dim), axis, backward)
        block = jnp.concatenate([low, block, high], axis=dim)
    return block


def on_device(
    features, new_owner, rim_rows, rim_counts, tile_sources, tile_values, w_self, w_neigh, cotangent
):
    rows = features.shape[2]
    width = features.shape[3]
    blocks = new_owner.shape[2]
    peers = lax.axis_size("dom")
    slots = 2 * blocks // peers
    block_rows = rows // blocks
    owner = new_owner[0, 0, :, 0]
    order = jnp.arange(blocks)
    same = owner[:, None] == owner[None, :]
    earlier = order[None, :] < order[:, None]
    rank = jnp.sum(jnp.where(same & earlier, 1, 0), axis=1).astype(jnp.int32)
    place = owner * slots + rank
    pieces = features[0, 0].reshape(blocks, block_rows * width)
    outbox = jnp.zeros((peers * slots, block_rows * width), jnp.bfloat16).at[place].set(pieces)
    inbox = lax.all_to_all(
        outbox.reshape(peers, slots * block_rows * width),
        "dom",
        split_axis=0,
        concat_axis=0,
        tiled=True,
    )
    owned = inbox.reshape(-1, width)
    rim_size = rim_rows.shape[3]
    picked = owned[rim_rows[0, 0]]
    valid = jnp.arange(rim_size)[None, :] < rim_counts[0, 0][:, None]
    outgoing = jnp.where(valid[:, :, None], picked, jnp.zeros_like(picked))
    along_dom = padded(jnp.concatenate([outgoing[1], outgoing[0]], axis=0), (("dom", 0),), rim_size)
    along_group = padded(
        jnp.concatenate([outgoing[3], outgoing[2]], axis=0), (("group", 0),), rim_size
    )
    extended = jnp.concatenate(
        [
            owned,
            along_dom[:rim_size],
            along_dom[-rim_size:],
            along_group[:rim_size],
            along_group[-rim_size:],
        ],
        axis=0,
    )
    tile = tile_values.shape[-1]
    tiles = extended.reshape(-1, tile, width)
    chosen = tiles[tile_sources[0, 0]]
    summed = jnp.einsum(
        "itab,itbf->iaf", tile_values[0, 0], chosen, preferred_element_type=jnp.float32
    )
    neigh = summed.reshape(-1, width).astype(jnp.bfloat16)
    pre = jnp.dot(owned, w_self, preferred_element_type=jnp.float32) + jnp.dot(
        neigh, w_neigh, preferred_element_type=jnp.float32
    )
    sig = jax.nn.sigmoid(pre)
    layer_out = (pre * sig).astype(jnp.bfloat16)
    dpre = (cotangent[0, 0].astype(jnp.float32) * sig * (1.0 + pre * (1.0 - sig))).astype(
        jnp.bfloat16
    )
    dims = (((0,), (0,)), ((), ()))
    g_self = lax.dot_general(owned, dpre, dims, preferred_element_type=jnp.float32)
    g_neigh = lax.dot_general(neigh, dpre, dims, preferred_element_type=jnp.float32)
    nodes = rows * peers * lax.axis_size("group")
    scale = 1.0 / jnp.sqrt(jnp.float32(nodes))
    sum_self, sum_neigh = lax.psum((g_self, g_neigh), ("dom", "group"))
    return (layer_out[None, None], sum_self * scale, sum_neigh * scale)


def solution(mesh):
    return jax.shard_map(
        on_device,
        mesh=mesh,
        in_specs=(
            P("group", "dom", None, None),
            P("group", "dom", None, None),
            P("group", "dom", None, None),
            P("group", "dom", None),
            P("group", "dom", None, None),
            P("group", "dom", None, None, None, None),
            P(),
            P(),
            P("group", "dom", None, None),
        ),
        out_specs=(P("group", "dom", None, None), P(), P()),
        check_vma=False,
    )
```

profile of v0, /device:TPU:1, one launch (start us, length us, event | category | flops | bytes accessed | tf_op | source)
XLA Modules:
  0.0 378.5 jit_solution(16374064793173778068)
XLA Ops:
  7.2 1.2 reshape.154
  8.3 0.9 select_reduce_fusion
  9.3 0.7 fusion.9
  9.9 1.2 scatter_custom_fusion
  11.1 0.9 all_to_all.8
  12.0 0.5 broadcast.87
  12.5 3.8 %reduce.1 = bf16[64,4096]{1,0:T(8,128)(2,1)S(1)} reduce(bf16[64,1,4096]{2,1,0:T(2,128)(2,1)S(1)} %all_to_all.8, bf16[]{:T(256)} %broadcast.87), dimensions={1}, to_apply=%all_to_all.8.reduce_sub_computation | reduce | bytes 1048578 | tf_op jit(solution)/shard_map/all_to_all | solution.py:38
  16.3 1.2 reshape.164
  17.5 14.0 %all-to-all-start = ((bf16[64,2,2048]{2,1,0:T(2,128)(2,1)}), bf16[64,2,2048]{2,1,0:T(2,128)(2,1)S(1)}, u32[]{:S(2)}, u32[]{:S(2)}) async-start(bf16[64,2,2048]{2,1,0:T(2,128)(2,1)} %reshape.164), calls=%async_computation | async-start | bytes 1048576 | tf_op jit(solution)/shard_map/all_to_all | solution.py:38
  31.5 0.0 all-reduce.3.cloned.1.call-start
  31.6 0.1 copy.18
  31.7 0.1 reshape.144
  31.8 0.1 iota_compare_fusion.1
  31.9 14.1 %all-to-all-done = bf16[64,2,2048]{2,1,0:T(2,128)(2,1)S(1)} async-done(((bf16[64,2,2048]{2,1,0:T(2,128)(2,1)}), bf16[64,2,2048]{2,1,0:T(2,128)(2,1)S(1)}, u32[]{:S(2)}, u32[]{:S(2)}) %all-to-all-start) | async-done | bytes 524320 | tf_op jit(solution)/shard_map/all_to_all | solution.py:38
  46.0 0.5 reshape.165
  46.5 3.1 reduce
  49.7 0.2 reshape.131
  50.0 2.0 gather_fusion
  51.9 0.1 broadcast_select_fusion
  52.1 3.1 collective-permute-start
  55.2 5.5 %collective-permute-start.1 = (bf16[128,256]{1,0:T(8,128)(2,1)S(1)}, bf16[128,256]{1,0:T(8,128)(2,1)S(1)}, u32[]{:S(2)}, u32[]{:S(2)}) collective-permute-start(bf16[128,256]{1,0:T(8,128)(2,1)S(1)} %get-tuple-element.9), channel_id=1, source_target_pairs={{16,0},{32,16},{48,32},{64,48},{80,64},{96,80},{112,96},{128,112},... | collective-permute-start | bytes 196616 | tf_op jit(solution)/shard_map/ppermute | solution.py:16
  60.7 9.7 %collective-permute-start.2 = (bf16[128,256]{1,0:T(8,128)(2,1)S(1)}, bf16[128,256]{1,0:T(8,128)(2,1)S(1)}, u32[]{:S(2)}, u32[]{:S(2)}) collective-permute-start(bf16[128,256]{1,0:T(8,128)(2,1)S(1)} %get-tuple-element.8), channel_id=1, source_target_pairs={{0,1},{1,2},{2,3},{3,4},{4,5},{5,6},{6,7},{7,8},{8,9},{9,10},{10,1... | collective-permute-start | bytes 196616 | tf_op jit(solution)/shard_map/ppermute | solution.py:13
  70.4 0.3 fusion.10
  70.8 0.9 collective-permute-done.2
  71.7 2.4 collective-permute-done.3
  74.1 2.0 gather_fusion.1
  76.1 2.2 fusion
  78.3 1.5 fusion.2
  79.8 1.0 fusion.12
  80.8 1.0 fusion.11
  81.9 288.0 %all-reduce.3.cloned.1.call-done = (f32[256,256]{1,0:T(8,128)}, f32[256,256]{1,0:T(8,128)}) async-done(((f32[256,256]{1,0:T(8,128)}, f32[256,256]{1,0:T(8,128)}), (f32[256,256]{1,0:T(8,128)}, f32[256,256]{1,0:T(8,128)})) %all-reduce.3.cloned.1.call-update) | async-done | bytes 524304 | tf_op jit(solution)/shard_map/psum | solution.py:84
  369.8 1.9 broadcast_multiply_fusion
  (28 shorter events, 0.2 us)
Async XLA Ops:
  7.2 68.9 %copy-start = (bf16[1,1,8,4,128,128]{5,4,3,2,1,0:T(8,128)(2,1)S(1)}, bf16[1,1,8,4,128,128]{5,4,3,2,1,0:T(8,128)(2,1)}, u32[]{:S(2)}) copy-start(bf16[1,1,8,4,128,128]{5,4,3,2,1,0:T(8,128)(2,1)} %param.14) | copy-start | bytes 3145732
  12.0 19.6 %copy-start.2 = (s32[1,1,8,4]{2,3,1,0:T(4,128)S(1)}, s32[1,1,8,4]{2,3,1,0:T(4,128)}, u32[]{:S(2)}) copy-start(s32[1,1,8,4]{2,3,1,0:T(4,128)} %param.13) | copy-start | bytes 388
  12.0 19.8 %copy-start.3 = (s32[1,1,4,128]{3,2,1,0:T(4,128)S(1)}, s32[1,1,4,128]{3,2,1,0:T(4,128)}, u32[]{:S(2)}) copy-start(s32[1,1,4,128]{3,2,1,0:T(4,128)} %param.11) | copy-start | bytes 6148
  12.0 19.8 %copy-start.6 = (s32[1,1,4]{2,1,0:T(1,128)S(1)}, s32[1,1,4]{2,1,0:T(1,128)}, u32[]{:S(2)}) copy-start(s32[1,1,4]{2,1,0:T(1,128)} %param.12) | copy-start | bytes 52
  17.5 28.5 %all-to-all-start = ((bf16[64,2,2048]{2,1,0:T(2,128)(2,1)}), bf16[64,2,2048]{2,1,0:T(2,128)(2,1)S(1)}, u32[]{:S(2)}, u32[]{:S(2)}) async-start(bf16[64,2,2048]{2,1,0:T(2,128)(2,1)} %reshape.164), calls=%async_computation | async-start | bytes 1048576 | tf_op jit(solution)/shard_map/all_to_all | solution.py:38
  31.5 338.3 %all-reduce.3.cloned.1.call-start = ((), (), s32[]{:S(2)}) async-start(), calls=%async_computation.1 | async-start | bytes 1048576 | tf_op jit(solution)/shard_map/psum | solution.py:84
  49.7 20.7 %copy-start.1 = (bf16[256,256]{1,0:T(8,128)(2,1)S(1)}, bf16[256,256]{1,0:T(8,128)(2,1)}, u32[]{:S(2)}) copy-start(bf16[256,256]{1,0:T(8,128)(2,1)} %param.15) | copy-start | bytes 393220
  52.1 18.6 %collective-permute-start = (bf16[128,256]{1,0:T(8,128)(2,1)S(1)}, bf16[128,256]{1,0:T(8,128)(2,1)S(1)}, u32[]{:S(2)}, u32[]{:S(2)}) collective-permute-start(bf16[128,256]{1,0:T(8,128)(2,1)S(1)} %get-tuple-element.10), channel_id=1, source_target_pairs={{0,16},{16,32},{32,48},{48,64},{64,80},{80,96},{96,112},{112,128},... | collective-permute-start | bytes 196616 | tf_op jit(solution)/shard_map/ppermute | solution.py:13
  55.2 15.5 %collective-permute-start.1 = (bf16[128,256]{1,0:T(8,128)(2,1)S(1)}, bf16[128,256]{1,0:T(8,128)(2,1)S(1)}, u32[]{:S(2)}, u32[]{:S(2)}) collective-permute-start(bf16[128,256]{1,0:T(8,128)(2,1)S(1)} %get-tuple-element.9), channel_id=1, source_target_pairs={{16,0},{32,16},{48,32},{64,48},{80,64},{96,80},{112,96},{128,112},... | collective-permute-start | bytes 196616 | tf_op jit(solution)/shard_map/ppermute | solution.py:16
  60.7 11.0 %collective-permute-start.2 = (bf16[128,256]{1,0:T(8,128)(2,1)S(1)}, bf16[128,256]{1,0:T(8,128)(2,1)S(1)}, u32[]{:S(2)}, u32[]{:S(2)}) collective-permute-start(bf16[128,256]{1,0:T(8,128)(2,1)S(1)} %get-tuple-element.8), channel_id=1, source_target_pairs={{0,1},{1,2},{2,3},{3,4},{4,5},{5,6},{6,7},{7,8},{8,9},{9,10},{10,1... | collective-permute-start | bytes 196616 | tf_op jit(solution)/shard_map/ppermute | solution.py:13
  70.4 3.7 collective-permute-start.3
  76.1 2.2 copy-start.4
  76.1 2.2 copy-start.5
Sparse Core Ops, SparseCore 0:
  82.0 287.7 all-reduce.2
where the time goes:
time: 379 us
  waiting for transfers between devices  305 us (80%)
  starting transfers between devices  32.3 us (9%)
  between operations  14.3 us (4%)
  other arithmetic  10.6 us (3%)
  local copies, waits for them, and re-layouts  9.91 us (3%)
  matrix products  5.99 us (2%)
    psum x1, waiting for transfers between devices, on_device(): sum_self, sum_neigh = lax.psum((g_self, g_neigh), ('dom', 'group'))  288 us
    all_to_all x1, waiting for transfers between devices, on_device(): lax.all_to_all(outbox.reshape(peers, slots * block_rows * width), 'dom',...  14.1 us
    all_to_all x1, starting transfers between devices, on_device(): lax.all_to_all(outbox.reshape(peers, slots * block_rows * width), 'dom',...  14 us
    ppermute x2, starting transfers between devices, padded(): lax.ppermute(lax.slice_in_dim(block, block.shape[dim] - width, None, axis...  12.8 us
  transfers between devices with their start and end apart: 6, of which 4 were waited for; matrix products, arithmetic and copies ran while one was open for 0% of the time, Pallas kernels for 0%

commit v1 on v0

v1 whole, which is shorter than its diff:
```python
import functools
import math

import jax
import jax.numpy as jnp
from jax import lax
from jax.experimental import pallas as pl
from jax.experimental.pallas import tpu as pltpu
from jax.sharding import PartitionSpec as P

F32 = jnp.float32
BF16 = jnp.bfloat16
I32 = jnp.int32
SIDE = 8
TILE = 128
RB = 8
CONTRACT_ROWS = (((0,), (0,)), ((), ()))


def iota(shape, axis):
    return lax.broadcasted_iota(I32, shape, axis)


def to_column(row, n):
    grid = jnp.where(iota((n, n), 0) == iota((n, n), 1), jnp.broadcast_to(row, (n, n)), 0)
    return jnp.sum(grid, axis=1, keepdims=True)


def kernel(
    scale,
    feat_hbm,
    owner_hbm,
    rim_hbm,
    cnt_hbm,
    src_hbm,
    val_hbm,
    ws_hbm,
    wn_hbm,
    cot_hbm,
    out_hbm,
    gs_hbm,
    gn_hbm,
    feat,
    owner,
    rim,
    cnt,
    src,
    val,
    ws,
    wn,
    cot,
    out,
    outbox,
    ext,
    pick,
    rim_out,
    x_t,
    pre_self,
    dpre,
    g_out,
    g_in,
    part,
    recv_a,
    red_a,
    recv_b,
    recv_z,
    recv_c,
    gat_b,
    gat_a,
    total,
    grad,
    in_sems,
    out_sems,
    a2a_send,
    a2a_recv,
    rim_send,
    rim_recv,
    ph_send,
    ph_recv,
):
    dom = lax.axis_index("dom")
    group = lax.axis_index("group")
    my_x, my_y = lax.rem(dom, SIDE), lax.div(dom, SIDE)
    my_z, core = lax.div(group, 2), lax.rem(group, 2)
    peers = SIDE * SIDE
    n_group = 2 * SIDE
    other = group + 1 - 2 * core

    loads = []
    for k, (a, b) in enumerate(
        (
            (owner_hbm, owner),
            (feat_hbm, feat),
            (rim_hbm, rim),
            (cnt_hbm, cnt),
            (src_hbm, src),
            (ws_hbm, ws),
            (wn_hbm, wn),
            (val_hbm, val),
            (cot_hbm, cot),
        )
    ):
        loads.append(pltpu.make_async_copy(a, b, in_sems.at[k]))
        loads[-1].start()
    l_owner, l_feat, l_rim, l_cnt, l_src, l_ws, l_wn, l_val, l_cot = loads

    barrier = pltpu.get_barrier_semaphore()

    def greet_dom(i, c):
        pl.semaphore_signal(
            barrier, inc=1, device_id={"dom": lax.rem(dom + i, peers), "group": group}
        )
        return c

    lax.fori_loop(1, peers, greet_dom, 0)

    def greet_z(i, c):
        pl.semaphore_signal(
            barrier,
            inc=1,
            device_id={"dom": dom, "group": lax.rem(my_z + i, SIDE) * 2 + core},
        )
        return c

    lax.fori_loop(1, SIDE, greet_z, 0)
    group_next = lax.rem(group + 1, n_group)
    group_prev = lax.rem(group + n_group - 1, n_group)
    for g in (group_next, group_prev):
        pl.semaphore_signal(barrier, inc=1, device_id={"dom": dom, "group": g})

    blocks = owner.shape[1]
    rows = feat.shape[0]
    l_owner.wait()
    owner_col = to_column(owner[...], blocks)
    block_of = lax.div(iota((blocks, rows), 1), RB)
    block_id = iota((blocks, rows), 0)
    owner_b = jnp.broadcast_to(owner_col, (blocks, rows))
    owner_row = jnp.sum(jnp.where(block_id == block_of, owner_b, 0), axis=0, keepdims=True)
    before = (owner_b == jnp.broadcast_to(owner_row, (blocks, rows))) & (block_id < block_of)
    rank = jnp.sum(jnp.where(before, 1, 0), axis=0, keepdims=True)
    slot_row = (owner_row * 2 + rank) * RB + lax.rem(iota((1, rows), 1), RB)

    l_feat.wait()
    share = 2 * RB
    for j in range(SIDE):
        yj = lax.rem(my_y + j, SIDE)
        hot = jnp.where(
            iota((TILE, rows), 0) + yj * TILE == jnp.broadcast_to(slot_row, (TILE, rows)),
            1.0,
            0.0,
        ).astype(BF16)
        outbox[yj] = jnp.dot(hot, feat[...], preferred_element_type=F32).astype(BF16)
        if j == 0:
            pl.semaphore_wait(barrier, peers - 1 + SIDE - 1 + 2)
            mine = pltpu.make_async_copy(
                outbox.at[my_y, pl.ds(my_x * share, share)],
                ext.at[my_y, pl.ds(my_x * share, share)],
                a2a_recv,
            )
            mine.start()

        def send(i, c, yj=yj):
            xi = lax.rem(my_x + i, SIDE)
            pltpu.make_async_remote_copy(
                src_ref=outbox.at[yj, pl.ds(xi * share, share)],
                dst_ref=ext.at[my_y, pl.ds(my_x * share, share)],
                send_sem=a2a_send,
                recv_sem=a2a_recv,
                device_id={"dom": yj * SIDE + xi, "group": group},
            ).start()
            return c

        lax.fori_loop(1 if j == 0 else 0, SIDE, send, 0)

    l_rim.wait()
    l_cnt.wait()
    n_rows = SIDE * TILE
    for p in range(4):
        column = to_column(rim[p : p + 1, :], TILE)
        column = jnp.where(iota((TILE, 1), 0) < cnt[0, p], column, -1)
        pick[p] = jnp.where(
            iota((TILE, n_rows), 1) == jnp.broadcast_to(column, (TILE, n_rows)), 1.0, 0.0
        ).astype(BF16)
    l_ws.wait()
    l_wn.wait()
    l_src.wait()
    l_val.wait()
    l_cot.wait()

    whole = ext.at[pl.ds(0, SIDE)]
    pltpu.make_async_copy(whole, whole, a2a_recv).wait()

    rims = (
        (0, {"dom": lax.rem(dom + 1, peers), "group": group}),
        (1, {"dom": lax.rem(dom + peers - 1, peers), "group": group}),
        (2, {"dom": dom, "group": group_next}),
        (3, {"dom": dom, "group": group_prev}),
    )
    owned = ext[0:SIDE].reshape(n_rows, feat.shape[1])
    rim_copies = []
    for p, target in rims:
        rim_out[p] = jnp.dot(pick[p], owned, preferred_element_type=F32).astype(BF16)
        rim_copies.append(
            pltpu.make_async_remote_copy(
                src_ref=rim_out.at[p],
                dst_ref=ext.at[SIDE + p],
                send_sem=rim_send.at[p],
                recv_sem=rim_recv.at[p],
                device_id=target,
            )
        )
        rim_copies[-1].start()
    for i in range(SIDE):
        tile = ext[i]
        x_t[0, :, i * TILE : (i + 1) * TILE] = tile.T
        pre_self[i] = jnp.dot(tile, ws[...], preferred_element_type=F32)
    for copy in rim_copies:
        copy.wait_recv()

    stores = []
    for i in range(SIDE):
        lhs = jnp.concatenate([val[i, t] for t in range(4)], axis=1)
        rhs = jnp.concatenate([ext[src[t, i]] for t in range(4)], axis=0)
        neigh = jnp.dot(lhs, rhs, preferred_element_type=F32).astype(BF16)
        x_t[1, :, i * TILE : (i + 1) * TILE] = neigh.T
        pre = pre_self[i] + jnp.dot(neigh, wn[...], preferred_element_type=F32)
        sig = jax.nn.sigmoid(pre)
        out[pl.ds(i * TILE, TILE), :] = (pre * sig).astype(BF16)
        dpre[pl.ds(i * TILE, TILE), :] = (
            cot[pl.ds(i * TILE, TILE), :].astype(F32) * sig * (1.0 + pre * (1.0 - sig))
        ).astype(BF16)
    store = pltpu.make_async_copy(out, out_hbm, out_sems.at[0])
    store.start()

    width = feat.shape[1]
    g_out[...] = jnp.dot(x_t[1 - core], dpre[...], preferred_element_type=F32)
    pair = pltpu.make_async_remote_copy(
        src_ref=g_out,
        dst_ref=g_in,
        send_sem=ph_send.at[0],
        recv_sem=ph_recv.at[0],
        device_id={"dom": dom, "group": other},
    )
    pair.start()
    own = jnp.dot(x_t[core], dpre[...], preferred_element_type=F32)
    pair.wait_recv()
    piece = width // SIDE
    part[...] = (own + g_in[...]).reshape(SIDE, piece, width)

    a, b = my_x + core * (my_y - my_x), my_y + core * (my_x - my_y)
    step_a, step_b = 1 + core * (SIDE - 1), SIDE - core * (SIDE - 1)

    def along(axis, k):
        if axis == "a":
            return {"dom": k * step_a + b * step_b, "group": group}
        if axis == "b":
            return {"dom": a * step_a + k * step_b, "group": group}
        return {"dom": dom, "group": k * 2 + core}

    def exchange(axis, me, phase, source, target):
        pltpu.make_async_copy(source(me), target.at[me], ph_recv.at[phase]).start()

        def send(i, c):
            k = lax.rem(me + i, SIDE)
            pltpu.make_async_remote_copy(
                src_ref=source(k),
                dst_ref=target.at[me],
                send_sem=ph_send.at[phase],
                recv_sem=ph_recv.at[phase],
                device_id=along(axis, k),
            ).start()
            return c

        lax.fori_loop(1, SIDE, send, 0)
        pltpu.make_async_copy(target, target, ph_recv.at[phase]).wait()

    exchange("a", a, 1, lambda k: part.at[k], recv_a)
    summed = jnp.sum(recv_a[...], axis=0)
    for k in range(SIDE):
        red_a[k] = summed[k // 2 * 8 : k // 2 * 8 + 8, k % 2 * TILE : k % 2 * TILE + TILE]
    exchange("b", b, 2, lambda k: red_a.at[k], recv_b)
    recv_c[...] = jnp.sum(recv_b[...], axis=0)
    exchange("z", my_z, 3, lambda k: recv_c, recv_z)
    recv_c2 = jnp.sum(recv_z[...], axis=0) * scale
    total[...] = recv_c2
    exchange("b", b, 4, lambda k: total, gat_b)
    exchange("a", a, 5, lambda k: gat_b, gat_a.at[core])
    back = pltpu.make_async_remote_copy(
        src_ref=gat_a.at[core],
        dst_ref=gat_a.at[core],
        send_sem=ph_send.at[6],
        recv_sem=ph_recv.at[6],
        device_id={"dom": dom, "group": other},
    )
    back.start()
    back.wait_recv()
    for w in range(2):
        for i in range(SIDE):
            for k in range(SIDE):
                r = i * piece + k // 2 * 8
                grad[w, r : r + 8, k % 2 * TILE : k % 2 * TILE + TILE] = gat_a[w, i, k]
    finals = [
        pltpu.make_async_copy(grad.at[0], gs_hbm, out_sems.at[1]),
        pltpu.make_async_copy(grad.at[1], gn_hbm, out_sems.at[2]),
    ]
    for copy in finals:
        copy.start()

    sent = outbox.at[pl.ds(0, SIDE - 1)]
    pltpu.make_async_copy(sent, sent, a2a_send).wait()
    rest = outbox.at[0, pl.ds(0, (SIDE - 1) * share)]
    pltpu.make_async_copy(rest, rest, a2a_send).wait()
    for copy in rim_copies:
        copy.wait_send()
    pair.wait_send()
    for phase, like in (
        (1, recv_a),
        (2, recv_b),
        (3, recv_z),
        (4, gat_b),
        (5, gat_a.at[0]),
    ):
        seven = like.at[pl.ds(0, SIDE - 1)]
        pltpu.make_async_copy(seven, seven, ph_send.at[phase]).wait()
    back.wait_send()
    store.wait()
    for copy in finals:
        copy.wait()


def on_device(
    features, new_owner, rim_rows, rim_counts, tile_sources, tile_values, w_self, w_neigh, cotangent
):
    rows, width = features.shape[2:]
    blocks = new_owner.shape[2]
    n_rows = cotangent.shape[2]
    hid = w_self.shape[1]
    nodes = rows * lax.axis_size("dom") * lax.axis_size("group")
    scale = 1.0 / math.sqrt(nodes)
    any_spec = pl.BlockSpec(memory_space=pl.ANY)
    out, g_self, g_neigh = pl.pallas_call(
        functools.partial(kernel, scale),
        out_shape=(
            jax.ShapeDtypeStruct((n_rows, hid), BF16),
            jax.ShapeDtypeStruct((width, hid), F32),
            jax.ShapeDtypeStruct((width, hid), F32),
        ),
        in_specs=[any_spec] * 9,
        out_specs=[any_spec] * 3,
        scratch_shapes=[
            pltpu.VMEM((rows, width), BF16),
            pltpu.VMEM((1, blocks), I32),
            pltpu.VMEM((4, TILE), I32),
            pltpu.SMEM((1, 4), I32),
            pltpu.SMEM((4, SIDE), I32),
            pltpu.VMEM((SIDE, 4, TILE, TILE), BF16),
            pltpu.VMEM((width, hid), BF16),
            pltpu.VMEM((width, hid), BF16),
            pltpu.VMEM((n_rows, hid), BF16),
            pltpu.VMEM((n_rows, hid), BF16),
            pltpu.VMEM((SIDE, TILE, width), BF16),
            pltpu.VMEM((SIDE + 4, TILE, width), BF16),
            pltpu.VMEM((4, TILE, n_rows), BF16),
            pltpu.VMEM((4, TILE, width), BF16),
            pltpu.VMEM((2, width, n_rows), BF16),
            pltpu.VMEM((SIDE, TILE, hid), F32),
            pltpu.VMEM((n_rows, hid), BF16),
            pltpu.VMEM((width, hid), F32),
            pltpu.VMEM((width, hid), F32),
            pltpu.VMEM((SIDE, width // SIDE, hid), F32),
            pltpu.VMEM((SIDE, width // SIDE, hid), F32),
            pltpu.VMEM((SIDE, 8, TILE), F32),
            pltpu.VMEM((SIDE, 8, TILE), F32),
            pltpu.VMEM((SIDE, 8, TILE), F32),
            pltpu.VMEM((8, TILE), F32),
            pltpu.VMEM((SIDE, 8, TILE), F32),
            pltpu.VMEM((2, SIDE, SIDE, 8, TILE), F32),
            pltpu.VMEM((8, TILE), F32),
            pltpu.VMEM((2, width, hid), F32),
            pltpu.SemaphoreType.DMA((9,)),
            pltpu.SemaphoreType.DMA((3,)),
            pltpu.SemaphoreType.DMA,
            pltpu.SemaphoreType.DMA,
            pltpu.SemaphoreType.DMA((4,)),
            pltpu.SemaphoreType.DMA((4,)),
            pltpu.SemaphoreType.DMA((7,)),
            pltpu.SemaphoreType.DMA((7,)),
        ],
        compiler_params=pltpu.CompilerParams(
            collective_id=0, has_side_effects=True, vmem_limit_bytes=48 * 1024 * 1024
        ),
    )(
        features[0, 0],
        new_owner[0, 0, :, 0][None],
        rim_rows[0, 0],
        rim_counts[0],
        tile_sources[0, 0].T,
        tile_values[0, 0],
        w_self,
        w_neigh,
        cotangent[0, 0],
    )
    return (out[None, None], g_self, g_neigh)


def solution(mesh):
    return jax.shard_map(
        on_device,
        mesh=mesh,
        in_specs=(
            P("group", "dom", None, None),
            P("group", "dom", None, None),
            P("group", "dom", None, None),
            P("group", "dom", None),
            P("group", "dom", None, None),
            P("group", "dom", None, None, None, None),
            P(),
            P(),
            P("group", "dom", None, None),
        ),
        out_specs=(P("group", "dom", None, None), P(), P()),
        check_vma=False,
    )
```

time: 379 us -> 92 us (0.24)
  waiting for transfers between devices: 305 us -> 0 us
  Pallas kernels: 0 us -> 83.1 us
  starting transfers between devices: 32.3 us -> 0 us
  between operations: 14.3 us -> 0.68 us
  other arithmetic: 10.6 us -> 0 us
  matrix products: 5.99 us -> 0 us
    psum x1 -> x0, waiting for transfers between devices: 288 us -> none  [on_device(): sum_self, sum_neigh = lax.psum((g_self, g_neigh), ('dom', 'group'))]
    pallas_call x0 -> x1, Pallas kernels: none -> 83.1 us  [on_device(): pl.pallas_call(functools.partial(kernel, scale), out_shape=(jax.ShapeDtyp...]
    ppermute x4 -> x0, starting transfers between devices: 18.3 us -> none  [the longest x2 12.8 us: padded(): lax.ppermute(lax.slice_in_dim(block, block.shape[dim] - width, None, axis...]
    all_to_all x1 -> x0, waiting for transfers between devices: 14.1 us -> none  [on_device(): lax.all_to_all(outbox.reshape(peers, slots * block_rows * width), 'dom',...]
    all_to_all x1 -> x0, starting transfers between devices: 14 us -> none  [on_device(): lax.all_to_all(outbox.reshape(peers, slots * block_rows * width), 'dom',...]
    all_to_all x2 -> x0, other arithmetic: 6.94 us -> none  [on_device(): lax.all_to_all(outbox.reshape(peers, slots * block_rows * width), 'dom',...]
    unnamed x20 -> x21, local copies, waits for them, and re-layouts: 1.79 us -> 7.89 us
    dot_general x5 -> x0, matrix products: 5.99 us -> none  [the longest x1 2.16 us: on_device(): jnp.einsum('itab,itbf->iaf', tile_values[0, 0], chosen, preferred_element...]
  transfers between devices with their start and end apart: 6 -> 0, of which waited for: 4 -> 0; matrix products, arithmetic and copies ran while one was open for 0% -> 0% of each run, Pallas kernels for 0% -> 0%
where the time goes in v1:
time: 92 us; the launch traced here: 91.7 us
  Pallas kernels  83.1 us (90%)
  local copies, waits for them, and re-layouts  7.89 us (9%)
    pallas_call x1, Pallas kernels, on_device(): pl.pallas_call(functools.partial(kernel, scale), out_shape=(jax.ShapeDtyp...  83.1 us
    unnamed x21, local copies, waits for them, and re-layouts  7.89 us

profile of v1, /device:TPU:1, one launch (start us, length us, event | category | flops | bytes accessed | tf_op | source)
XLA Modules:
  0.0 91.7 jit_solution(806302048570795324)
XLA Ops:
  0.6 0.0 copy-start.6
  0.6 0.0 copy-start.5
  0.7 0.0 copy-start.7
  0.7 0.0 copy-start.8
  0.7 0.6 copy-done.6
  1.3 0.0 copy-done.5
  1.3 0.0 copy-done.7
  1.3 0.0 copy-done.8
  1.3 0.0 copy-start
  1.3 1.2 %copy-done = bf16[1,1,8,4,128,128]{5,4,3,2,1,0:T(8,128)(2,1)S(1)} copy-done((bf16[1,1,8,4,128,128]{5,4,3,2,1,0:T(8,128)(2,1)S(1)}, bf16[1,1,8,4,128,128]{5,4,3,2,1,0:T(8,128)(2,1)}, u32[]{:S(2)}) %copy-start) | copy-done | bytes 1048600
  2.6 0.0 copy-start.1
  2.6 1.0 %copy-done.1 = bf16[1,1,1024,256]{3,2,1,0:T(8,128)(2,1)S(1)} copy-done((bf16[1,1,1024,256]{3,2,1,0:T(8,128)(2,1)S(1)}, bf16[1,1,1024,256]{3,2,1,0:T(8,128)(2,1)}, u32[]{:S(2)}) %copy-start.1) | copy-done | bytes 524312
  3.6 0.0 copy-start.2
  3.6 0.9 %copy-done.2 = bf16[1,1,512,256]{3,2,1,0:T(8,128)(2,1)S(1)} copy-done((bf16[1,1,512,256]{3,2,1,0:T(8,128)(2,1)S(1)}, bf16[1,1,512,256]{3,2,1,0:T(8,128)(2,1)}, u32[]{:S(2)}) %copy-start.2) | copy-done | bytes 262168
  4.6 0.0 copy-start.3
  4.6 0.9 copy-done.3
  5.5 0.0 copy-start.4
  5.5 0.9 copy-done.4
  6.4 83.1 %shard_map.112 = (bf16[1024,256]{1,0:T(8,128)(2,1)S(1)}, f32[256,256]{1,0:T(8,128)S(1)}, f32[256,256]{1,0:T(8,128)S(1)}) custom-call(bf16[512,256]{1,0:T(8,128)(2,1)S(1)} %bitcast.13, s32[1,64]{1,0:T(1,128)S(1)} %bitcast.16, s32[4,128]{1,0:T(4,128)S(1)} %bitcast.14, s32[1,4]{1,0:T(1,128)S(1)} %bitcast.17, s32[4,8]{1,0:T(4,128)S(1)} %bitcast.15, ...), custom_call_target="tpu_custom_call" | custom-call | tf_op jit(solution)/shard_map/pallas_call | solution.py:341
  89.5 0.8 copy.15
  90.3 0.7 copy.16
  91.0 0.7 copy.17
Async XLA Ops:
  0.6 0.7 copy-start.6
  0.6 0.7 copy-start.5
  0.7 0.7 copy-start.7
  0.7 0.7 copy-start.8
  1.3 1.2 %copy-start = (bf16[1,1,8,4,128,128]{5,4,3,2,1,0:T(8,128)(2,1)S(1)}, bf16[1,1,8,4,128,128]{5,4,3,2,1,0:T(8,128)(2,1)}, u32[]{:S(2)}) copy-start(bf16[1,1,8,4,128,128]{5,4,3,2,1,0:T(8,128)(2,1)} %param.14) | copy-start | bytes 3145732
  2.6 1.0 %copy-start.1 = (bf16[1,1,1024,256]{3,2,1,0:T(8,128)(2,1)S(1)}, bf16[1,1,1024,256]{3,2,1,0:T(8,128)(2,1)}, u32[]{:S(2)}) copy-start(bf16[1,1,1024,256]{3,2,1,0:T(8,128)(2,1)} %param.17) | copy-start | bytes 1572868
  3.6 0.9 %copy-start.2 = (bf16[1,1,512,256]{3,2,1,0:T(8,128)(2,1)S(1)}, bf16[1,1,512,256]{3,2,1,0:T(8,128)(2,1)}, u32[]{:S(2)}) copy-start(bf16[1,1,512,256]{3,2,1,0:T(8,128)(2,1)} %param.9) | copy-start | bytes 786436
  4.6 0.9 copy-start.3
  5.5 0.9 copy-start.4

commit v2 on v1

--- a/solution.py
+++ b/solution.py
@@ -14,7 +14,21 @@
 SIDE = 8
 TILE = 128
 RB = 8
-CONTRACT_ROWS = (((0,), (0,)), ((), ()))
+PIECES = SIDE * SIDE // 2
+Z_STEPS = (4, 3, 5, 2, 6, 1, 7)
+VMEM_LIMIT = 48 * 1024 * 1024
+
+
+def ring(d):
+    return min(d, SIDE - d)
+
+
+STEPS = sorted(
+    ((dx, dy) for dy in range(SIDE) for dx in range(SIDE) if dx or dy),
+    key=lambda s: -ring(s[0]) - ring(s[1]),
+)
+EVEN = [s for s in STEPS if sum(s) % 2 == 0] + [(0, 0)]
+ODD = [s for s in STEPS if sum(s) % 2 == 1]
 
 
 def iota(shape, axis):
@@ -37,9 +51,8 @@
     ws_hbm,
     wn_hbm,
     cot_hbm,
-    out_hbm,
-    gs_hbm,
-    gn_hbm,
+    out_any,
+    gath,
     feat,
     owner,
     rim,
@@ -60,17 +73,12 @@
     g_out,
     g_in,
     part,
-    recv_a,
-    red_a,
-    recv_b,
+    recv,
+    z_part,
     recv_z,
-    recv_c,
-    gat_b,
-    gat_a,
     total,
-    grad,
     in_sems,
-    out_sems,
+    out_sem,
     a2a_send,
     a2a_recv,
     rim_send,
@@ -86,6 +94,11 @@
     n_group = 2 * SIDE
     other = group + 1 - 2 * core
 
+    pending = []
+
+    def wait_for(like, sem):
+        pltpu.make_async_copy(like, like, sem).wait()
+
     loads = []
     for k, (a, b) in enumerate(
         (
@@ -143,34 +156,29 @@
     l_feat.wait()
     share = 2 * RB
     for j in range(SIDE):
-        yj = lax.rem(my_y + j, SIDE)
         hot = jnp.where(
-            iota((TILE, rows), 0) + yj * TILE == jnp.broadcast_to(slot_row, (TILE, rows)),
+            iota((TILE, rows), 0) + j * TILE == jnp.broadcast_to(slot_row, (TILE, rows)),
             1.0,
             0.0,
         ).astype(BF16)
-        outbox[yj] = jnp.dot(hot, feat[...], preferred_element_type=F32).astype(BF16)
-        if j == 0:
-            pl.semaphore_wait(barrier, peers - 1 + SIDE - 1 + 2)
-            mine = pltpu.make_async_copy(
-                outbox.at[my_y, pl.ds(my_x * share, share)],
-                ext.at[my_y, pl.ds(my_x * share, share)],
-                a2a_recv,
-            )
-            mine.start()
-
-        def send(i, c, yj=yj):
-            xi = lax.rem(my_x + i, SIDE)
-            pltpu.make_async_remote_copy(
-                src_ref=outbox.at[yj, pl.ds(xi * share, share)],
-                dst_ref=ext.at[my_y, pl.ds(my_x * share, share)],
-                send_sem=a2a_send,
-                recv_sem=a2a_recv,
-                device_id={"dom": yj * SIDE + xi, "group": group},
-            ).start()
-            return c
-
-        lax.fori_loop(1 if j == 0 else 0, SIDE, send, 0)
+        outbox[j] = jnp.dot(hot, feat[...], preferred_element_type=F32).astype(BF16)
+    pl.semaphore_wait(barrier, peers - 1 + SIDE - 1 + 2)
+    for dx, dy in STEPS:
+        xi, yi = lax.rem(my_x + dx, SIDE), lax.rem(my_y + dy, SIDE)
+        pltpu.make_async_remote_copy(
+            src_ref=outbox.at[yi, pl.ds(xi * share, share)],
+            dst_ref=ext.at[my_y, pl.ds(my_x * share, share)],
+            send_sem=a2a_send,
+            recv_sem=a2a_recv,
+            device_id={"dom": yi * SIDE + xi, "group": group},
+        ).start()
+    pltpu.make_async_copy(
+        outbox.at[my_y, pl.ds(my_x * share, share)],
+        ext.at[my_y, pl.ds(my_x * share, share)],
+        a2a_recv,
+    ).start()
+    pending.append(lambda: wait_for(outbox.at[pl.ds(0, SIDE - 1)], a2a_send))
+    pending.append(lambda: wait_for(outbox.at[0, pl.ds(0, (SIDE - 1) * share)], a2a_send))
 
     l_rim.wait()
     l_cnt.wait()
@@ -187,8 +195,7 @@
     l_val.wait()
     l_cot.wait()
 
-    whole = ext.at[pl.ds(0, SIDE)]
-    pltpu.make_async_copy(whole, whole, a2a_recv).wait()
+    wait_for(ext.at[pl.ds(0, SIDE)], a2a_recv)
 
     rims = (
         (0, {"dom": lax.rem(dom + 1, peers), "group": group}),
@@ -210,6 +217,7 @@
             )
         )
         rim_copies[-1].start()
+        pending.append(rim_copies[-1].wait_send)
     for i in range(SIDE):
         tile = ext[i]
         x_t[0, :, i * TILE : (i + 1) * TILE] = tile.T
@@ -229,8 +237,9 @@
         dpre[pl.ds(i * TILE, TILE), :] = (
             cot[pl.ds(i * TILE, TILE), :].astype(F32) * sig * (1.0 + pre * (1.0 - sig))
         ).astype(BF16)
-    store = pltpu.make_async_copy(out, out_hbm, out_sems.at[0])
+    store = pltpu.make_async_copy(out, out_any, out_sem)
     store.start()
+    pending.append(store.wait)
 
     width = feat.shape[1]
     g_out[...] = jnp.dot(x_t[1 - core], dpre[...], preferred_element_type=F32)
@@ -242,89 +251,98 @@
         device_id={"dom": dom, "group": other},
     )
     pair.start()
+    pending.append(pair.wait_send)
     own = jnp.dot(x_t[core], dpre[...], preferred_element_type=F32)
     pair.wait_recv()
-    piece = width // SIDE
-    part[...] = (own + g_in[...]).reshape(SIDE, piece, width)
-
-    a, b = my_x + core * (my_y - my_x), my_y + core * (my_x - my_y)
-    step_a, step_b = 1 + core * (SIDE - 1), SIDE - core * (SIDE - 1)
-
-    def along(axis, k):
-        if axis == "a":
-            return {"dom": k * step_a + b * step_b, "group": group}
-        if axis == "b":
-            return {"dom": a * step_a + k * step_b, "group": group}
-        return {"dom": dom, "group": k * 2 + core}
-
-    def exchange(axis, me, phase, source, target):
-        pltpu.make_async_copy(source(me), target.at[me], ph_recv.at[phase]).start()
-
-        def send(i, c):
-            k = lax.rem(me + i, SIDE)
+    summed = own + g_in[...]
+    for k in range(PIECES):
+        r, c = k // 2 * 16, k % 2 * TILE
+        part[k] = summed[r : r + 16, c : c + TILE].astype(BF16)
+
+    odd = lax.rem(my_x + my_y + core, 2)
+    mine = my_y * (SIDE // 2) + lax.div(my_x, 2)
+
+    def to_owner(dx, dy):
+        xi, yi = lax.rem(my_x + dx, SIDE), lax.rem(my_y + dy, SIDE)
+        return pltpu.make_async_remote_copy(
+            src_ref=part.at[yi * (SIDE // 2) + lax.div(xi, 2)],
+            dst_ref=recv.at[dom],
+            send_sem=ph_send.at[1],
+            recv_sem=ph_recv.at[1],
+            device_id={"dom": yi * SIDE + xi, "group": group},
+        )
+
+    for (ex, ey), (ox, oy) in zip(EVEN[:-1], ODD[:-1]):
+        to_owner(ex + odd * (ox - ex), ey + odd * (oy - ey)).start()
+
+    @pl.when(odd == 1)
+    def _():
+        to_owner(*ODD[-1]).start()
+
+    @pl.when(odd == 0)
+    def _():
+        pltpu.make_async_copy(part.at[mine], recv.at[dom], ph_recv.at[1]).start()
+        wait_for(recv, ph_recv.at[1])
+        z_part[...] = jnp.sum(recv[...].astype(F32), axis=0)
+
+        for i in Z_STEPS:
             pltpu.make_async_remote_copy(
-                src_ref=source(k),
-                dst_ref=target.at[me],
-                send_sem=ph_send.at[phase],
-                recv_sem=ph_recv.at[phase],
-                device_id=along(axis, k),
+                src_ref=z_part,
+                dst_ref=recv_z.at[my_z],
+                send_sem=ph_send.at[2],
+                recv_sem=ph_recv.at[2],
+                device_id={"dom": dom, "group": lax.rem(my_z + i, SIDE) * 2 + core},
             ).start()
-            return c
-
-        lax.fori_loop(1, SIDE, send, 0)
-        pltpu.make_async_copy(target, target, ph_recv.at[phase]).wait()
-
-    exchange("a", a, 1, lambda k: part.at[k], recv_a)
-    summed = jnp.sum(recv_a[...], axis=0)
-    for k in range(SIDE):
-        red_a[k] = summed[k // 2 * 8 : k // 2 * 8 + 8, k % 2 * TILE : k % 2 * TILE + TILE]
-    exchange("b", b, 2, lambda k: red_a.at[k], recv_b)
-    recv_c[...] = jnp.sum(recv_b[...], axis=0)
-    exchange("z", my_z, 3, lambda k: recv_c, recv_z)
-    recv_c2 = jnp.sum(recv_z[...], axis=0) * scale
-    total[...] = recv_c2
-    exchange("b", b, 4, lambda k: total, gat_b)
-    exchange("a", a, 5, lambda k: gat_b, gat_a.at[core])
+        pltpu.make_async_copy(z_part, recv_z.at[my_z], ph_recv.at[2]).start()
+        wait_for(recv_z, ph_recv.at[2])
+        total[...] = (jnp.sum(recv_z[...], axis=0) * scale).astype(BF16)
+
+        for dx, dy in STEPS:
+            xi, yi = lax.rem(my_x + dx, SIDE), lax.rem(my_y + dy, SIDE)
+            pltpu.make_async_remote_copy(
+                src_ref=total,
+                dst_ref=gath.at[core, mine],
+                send_sem=ph_send.at[3],
+                recv_sem=ph_recv.at[3],
+                device_id={"dom": yi * SIDE + xi, "group": group},
+            ).start()
+        pltpu.make_async_copy(total, gath.at[core, mine], ph_recv.at[3]).start()
+
+    wait_for(gath.at[core], ph_recv.at[3])
     back = pltpu.make_async_remote_copy(
-        src_ref=gat_a.at[core],
-        dst_ref=gat_a.at[core],
-        send_sem=ph_send.at[6],
-        recv_sem=ph_recv.at[6],
+        src_ref=gath.at[core],
+        dst_ref=gath.at[core],
+        send_sem=ph_send.at[4],
+        recv_sem=ph_recv.at[4],
         device_id={"dom": dom, "group": other},
     )
     back.start()
-    back.wait_recv()
-    for w in range(2):
-        for i in range(SIDE):
-            for k in range(SIDE):
-                r = i * piece + k // 2 * 8
-                grad[w, r : r + 8, k % 2 * TILE : k % 2 * TILE + TILE] = gat_a[w, i, k]
-    finals = [
-        pltpu.make_async_copy(grad.at[0], gs_hbm, out_sems.at[1]),
-        pltpu.make_async_copy(grad.at[1], gn_hbm, out_sems.at[2]),
-    ]
-    for copy in finals:
-        copy.start()
-
-    sent = outbox.at[pl.ds(0, SIDE - 1)]
-    pltpu.make_async_copy(sent, sent, a2a_send).wait()
-    rest = outbox.at[0, pl.ds(0, (SIDE - 1) * share)]
-    pltpu.make_async_copy(rest, rest, a2a_send).wait()
-    for copy in rim_copies:
-        copy.wait_send()
-    pair.wait_send()
-    for phase, like in (
-        (1, recv_a),
-        (2, recv_b),
-        (3, recv_z),
-        (4, gat_b),
-        (5, gat_a.at[0]),
-    ):
-        seven = like.at[pl.ds(0, SIDE - 1)]
-        pltpu.make_async_copy(seven, seven, ph_send.at[phase]).wait()
-    back.wait_send()
-    store.wait()
-    for copy in finals:
+
+    @pl.when(odd == 1)
+    def _():
+        wait_for(recv.at[pl.ds(0, PIECES)], ph_send.at[1])
+
+    @pl.when(odd == 0)
+    def _():
+        wait_for(recv.at[pl.ds(0, PIECES - 1)], ph_send.at[1])
+        wait_for(recv_z.at[pl.ds(0, SIDE - 1)], ph_send.at[2])
+        wait_for(recv.at[pl.ds(0, peers - 1)], ph_send.at[3])
+
+    for wait in pending:
+        wait()
+    back.wait()
+
+
+def finish(out_in, gath, out, g_self, g_neigh, grads, sems):
+    copies = [pltpu.make_async_copy(out_in, out, sems.at[2])]
+    copies[0].start()
+    for w, target in enumerate((g_self, g_neigh)):
+        for k in range(PIECES):
+            r, c = k // 2 * 16, k % 2 * TILE
+            grads[w, r : r + 16, c : c + TILE] = gath[w, k].astype(F32)
+        copies.append(pltpu.make_async_copy(grads.at[w], target, sems.at[w]))
+        copies[-1].start()
+    for copy in copies:
         copy.wait()
 
 
@@ -338,15 +356,14 @@
     nodes = rows * lax.axis_size("dom") * lax.axis_size("group")
     scale = 1.0 / math.sqrt(nodes)
     any_spec = pl.BlockSpec(memory_space=pl.ANY)
-    out, g_self, g_neigh = pl.pallas_call(
+    out, gath = pl.pallas_call(
         functools.partial(kernel, scale),
         out_shape=(
-            jax.ShapeDtypeStruct((n_rows, hid), BF16),
-            jax.ShapeDtypeStruct((width, hid), F32),
-            jax.ShapeDtypeStruct((width, hid), F32),
+            pltpu.VMEM((n_rows, hid), BF16),
+            pltpu.VMEM((2, PIECES, 16, TILE), BF16),
         ),
         in_specs=[any_spec] * 9,
-        out_specs=[any_spec] * 3,
+        out_specs=[any_spec] * 2,
         scratch_shapes=[
             pltpu.VMEM((rows, width), BF16),
             pltpu.VMEM((1, blocks), I32),
@@ -367,39 +384,51 @@
             pltpu.VMEM((n_rows, hid), BF16),
             pltpu.VMEM((width, hid), F32),
             pltpu.VMEM((width, hid), F32),
-            pltpu.VMEM((SIDE, width // SIDE, hid), F32),
-            pltpu.VMEM((SIDE, width // SIDE, hid), F32),
-            pltpu.VMEM((SIDE, 8, TILE), F32),
-            pltpu.VMEM((SIDE, 8, TILE), F32),
-            pltpu.VMEM((SIDE, 8, TILE), F32),
-            pltpu.VMEM((8, TILE), F32),
-            pltpu.VMEM((SIDE, 8, TILE), F32),
-            pltpu.VMEM((2, SIDE, SIDE, 8, TILE), F32),
-            pltpu.VMEM((8, TILE), F32),
-            pltpu.VMEM((2, width, hid), F32),
+            pltpu.VMEM((PIECES, 16, TILE), BF16),
+            pltpu.VMEM((SIDE * SIDE, 16, TILE), BF16),
+            pltpu.VMEM((16, TILE), F32),
+            pltpu.VMEM((SIDE, 16, TILE), F32),
+            pltpu.VMEM((16, TILE), BF16),
             pltpu.SemaphoreType.DMA((9,)),
-            pltpu.SemaphoreType.DMA((3,)),
+            pltpu.SemaphoreType.DMA,
             pltpu.SemaphoreType.DMA,
             pltpu.SemaphoreType.DMA,
             pltpu.SemaphoreType.DMA((4,)),
             pltpu.SemaphoreType.DMA((4,)),
-            pltpu.SemaphoreType.DMA((7,)),
-            pltpu.SemaphoreType.DMA((7,)),
+            pltpu.SemaphoreType.DMA((5,)),
+            pltpu.SemaphoreType.DMA((5,)),
         ],
         compiler_params=pltpu.CompilerParams(
-            collective_id=0, has_side_effects=True, vmem_limit_bytes=48 * 1024 * 1024
+            collective_id=0, has_side_effects=True, vmem_limit_bytes=VMEM_LIMIT
         ),
     )(
-        features[0, 0],
-        new_owner[0, 0, :, 0][None],
-        rim_rows[0, 0],
-        rim_counts[0],
-        tile_sources[0, 0].T,
-        tile_values[0, 0],
-        w_self,
-        w_neigh,
-        cotangent[0, 0],
+        *(
+            pltpu.with_memory_space_constraint(a, pltpu.HBM)
+            for a in (
+                features[0, 0],
+                new_owner[0, 0, :, 0][None],
+                rim_rows[0, 0],
+                rim_counts[0],
+                tile_sources[0, 0].T,
+                tile_values[0, 0],
+                w_self,
+                w_neigh,
+                cotangent[0, 0],
+            )
+        )
     )
+    out, g_self, g_neigh = pl.pallas_call(
+        finish,
+        out_shape=(
+            pltpu.HBM((n_rows, hid), BF16),
+            pltpu.HBM((width, hid), F32),
+            pltpu.HBM((width, hid), F32),
+        ),
+        in_specs=[any_spec, pl.BlockSpec(memory_space=pltpu.VMEM)],
+        out_specs=[any_spec] * 3,
+        scratch_shapes=[pltpu.VMEM((2, width, hid), F32), pltpu.SemaphoreType.DMA((3,))],
+        compiler_params=pltpu.CompilerParams(vmem_limit_bytes=VMEM_LIMIT),
+    )(out, gath)
     return (out[None, None], g_self, g_neigh)
 
 

time: 92 us -> 69.6 us (0.76)
  Pallas kernels: 83.1 us -> 68.8 us
  local copies, waits for them, and re-layouts: 7.89 us -> 0 us
    pallas_call x1 -> x2, Pallas kernels: 83.1 us -> 68.8 us  [the longest x1 67.9 us: on_device(): pl.pallas_call(functools.partial(kernel, scale), out_shape=(pltpu.VMEM((n...]
    unnamed x21 -> x0, local copies, waits for them, and re-layouts: 7.89 us -> none
where the time goes in v2:
time: 69.6 us; the launch traced here: 69.5 us
  Pallas kernels  68.8 us (99%)
    pallas_call x1, Pallas kernels, on_device(): pl.pallas_call(functools.partial(kernel, scale), out_shape=(pltpu.VMEM((n...  67.9 us

profile of v2, /device:TPU:1, one launch (start us, length us, event | category | flops | bytes accessed | tf_op | source)
XLA Modules:
  0.0 69.5 jit_solution(17694252350333855240)
XLA Ops:
  0.6 67.9 %shard_map.112 = (bf16[1024,256]{1,0:T(8,128)(2,1)S(1)}, bf16[2,32,16,128]{3,2,1,0:T(8,128)(2,1)S(1)}) custom-call(bf16[512,256]{1,0:T(8,128)(2,1)} %bitcast.12, s32[1,64]{1,0:T(1,128)} %bitcast.15, s32[4,128]{1,0:T(4,128)} %bitcast.13, s32[1,4]{1,0:T(1,128)} %bitcast.16, s32[4,8]{1,0:T(4,128)} %bitcast.14, bf16[8,4,128,128]{3,2,1,0:T(8,128)(2,1)} %bitcast.10, ...), custom_call_target="tpu_custom_call" | custom-call | tf_op jit(solution)/shard_map/pallas_call | solution.py:359
  68.5 1.0 %shard_map.113 = (bf16[1024,256]{1,0:T(8,128)(2,1)}, f32[256,256]{1,0:T(8,128)}, f32[256,256]{1,0:T(8,128)}) custom-call(bf16[1024,256]{1,0:T(8,128)(2,1)S(1)} %get-tuple-element.8.out_in, bf16[2,32,16,128]{3,2,1,0:T(8,128)(2,1)S(1)} %get-tuple-element.9.gath), custom_call_target="tpu_custom_call" | custom-call | tf_op jit(solution)/shard_map/pallas_call | solution.py:420

commit v3 on v2

--- a/solution.py
+++ b/solution.py
@@ -69,9 +69,11 @@
     rim_out,
     x_t,
     pre_self,
+    neighbours,
     dpre,
     g_out,
     g_in,
+    g_own,
     part,
     recv,
     z_part,
@@ -83,6 +85,8 @@
     a2a_recv,
     rim_send,
     rim_recv,
+    pair_send,
+    pair_recv,
     ph_send,
     ph_recv,
 ):
@@ -93,6 +97,18 @@
     peers = SIDE * SIDE
     n_group = 2 * SIDE
     other = group + 1 - 2 * core
+
+    barrier = pltpu.get_barrier_semaphore()
+    group_next = lax.rem(group + 1, n_group)
+    group_prev = lax.rem(group + n_group - 1, n_group)
+    along_z = [lax.rem(my_z + i, SIDE) * 2 + core for i in Z_STEPS]
+    for g in [*along_z, group_next, group_prev]:
+        pl.semaphore_signal(barrier, inc=1, device_id={"dom": dom, "group": g})
+    in_plane = []
+    for dx, dy in STEPS:
+        xi, yi = lax.rem(my_x + dx, SIDE), lax.rem(my_y + dy, SIDE)
+        in_plane.append((xi, yi, {"dom": yi * SIDE + xi, "group": group}))
+        pl.semaphore_signal(barrier, inc=1, device_id=in_plane[-1][2])
 
     pending = []
 
@@ -117,30 +133,6 @@
         loads[-1].start()
     l_owner, l_feat, l_rim, l_cnt, l_src, l_ws, l_wn, l_val, l_cot = loads
 
-    barrier = pltpu.get_barrier_semaphore()
-
-    def greet_dom(i, c):
-        pl.semaphore_signal(
-            barrier, inc=1, device_id={"dom": lax.rem(dom + i, peers), "group": group}
-        )
-        return c
-
-    lax.fori_loop(1, peers, greet_dom, 0)
-
-    def greet_z(i, c):
-        pl.semaphore_signal(
-            barrier,
-            inc=1,
-            device_id={"dom": dom, "group": lax.rem(my_z + i, SIDE) * 2 + core},
-        )
-        return c
-
-    lax.fori_loop(1, SIDE, greet_z, 0)
-    group_next = lax.rem(group + 1, n_group)
-    group_prev = lax.rem(group + n_group - 1, n_group)
-    for g in (group_next, group_prev):
-        pl.semaphore_signal(barrier, inc=1, device_id={"dom": dom, "group": g})
-
     blocks = owner.shape[1]
     rows = feat.shape[0]
     l_owner.wait()
@@ -163,14 +155,13 @@
         ).astype(BF16)
         outbox[j] = jnp.dot(hot, feat[...], preferred_element_type=F32).astype(BF16)
     pl.semaphore_wait(barrier, peers - 1 + SIDE - 1 + 2)
-    for dx, dy in STEPS:
-        xi, yi = lax.rem(my_x + dx, SIDE), lax.rem(my_y + dy, SIDE)
+    for xi, yi, target in in_plane:
         pltpu.make_async_remote_copy(
             src_ref=outbox.at[yi, pl.ds(xi * share, share)],
             dst_ref=ext.at[my_y, pl.ds(my_x * share, share)],
             send_sem=a2a_send,
             recv_sem=a2a_recv,
-            device_id={"dom": yi * SIDE + xi, "group": group},
+            device_id=target,
         ).start()
     pltpu.make_async_copy(
         outbox.at[my_y, pl.ds(my_x * share, share)],
@@ -219,9 +210,13 @@
         rim_copies[-1].start()
         pending.append(rim_copies[-1].wait_send)
     for i in range(SIDE):
-        tile = ext[i]
-        x_t[0, :, i * TILE : (i + 1) * TILE] = tile.T
-        pre_self[i] = jnp.dot(tile, ws[...], preferred_element_type=F32)
+        x_t[0, :, i * TILE : (i + 1) * TILE] = ext[i].T
+    quarter = n_rows // 4
+    for h in range(4):
+        r = pl.ds(h * quarter, quarter)
+        pre_self[r, :] = jnp.dot(
+            owned[h * quarter : (h + 1) * quarter], ws[...], preferred_element_type=F32
+        )
     for copy in rim_copies:
         copy.wait_recv()
 
@@ -229,35 +224,44 @@
     for i in range(SIDE):
         lhs = jnp.concatenate([val[i, t] for t in range(4)], axis=1)
         rhs = jnp.concatenate([ext[src[t, i]] for t in range(4)], axis=0)
-        neigh = jnp.dot(lhs, rhs, preferred_element_type=F32).astype(BF16)
-        x_t[1, :, i * TILE : (i + 1) * TILE] = neigh.T
-        pre = pre_self[i] + jnp.dot(neigh, wn[...], preferred_element_type=F32)
-        sig = jax.nn.sigmoid(pre)
-        out[pl.ds(i * TILE, TILE), :] = (pre * sig).astype(BF16)
-        dpre[pl.ds(i * TILE, TILE), :] = (
-            cot[pl.ds(i * TILE, TILE), :].astype(F32) * sig * (1.0 + pre * (1.0 - sig))
+        neighbours[pl.ds(i * TILE, TILE), :] = jnp.dot(
+            lhs, rhs, preferred_element_type=F32
         ).astype(BF16)
-    store = pltpu.make_async_copy(out, out_any, out_sem)
-    store.start()
-    pending.append(store.wait)
+    for h in range(4):
+        r = pl.ds(h * quarter, quarter)
+        neigh = neighbours[r, :]
+        x_t[1, :, h * quarter : (h + 1) * quarter] = neigh.T
+        pre = pre_self[r, :] + jnp.dot(neigh, wn[...], preferred_element_type=F32)
+        sig = 0.5 * jnp.tanh(0.5 * pre) + 0.5
+        silu = pre * sig
+        out[r, :] = silu.astype(BF16)
+        dpre[r, :] = (cot[r, :].astype(F32) * (sig + silu * (1.0 - sig))).astype(BF16)
 
     width = feat.shape[1]
-    g_out[...] = jnp.dot(x_t[1 - core], dpre[...], preferred_element_type=F32)
-    pair = pltpu.make_async_remote_copy(
-        src_ref=g_out,
-        dst_ref=g_in,
-        send_sem=ph_send.at[0],
-        recv_sem=ph_recv.at[0],
-        device_id={"dom": dom, "group": other},
-    )
-    pair.start()
-    pending.append(pair.wait_send)
-    own = jnp.dot(x_t[core], dpre[...], preferred_element_type=F32)
-    pair.wait_recv()
-    summed = own + g_in[...]
-    for k in range(PIECES):
-        r, c = k // 2 * 16, k % 2 * TILE
-        part[k] = summed[r : r + 16, c : c + TILE].astype(BF16)
+    half = width // 2
+    pairs = []
+    for h in range(2):
+        r = pl.ds(h * half, half)
+        g_out[r, :] = jnp.dot(x_t[1 - core, r, :], dpre[...], preferred_element_type=F32)
+        pairs.append(
+            pltpu.make_async_remote_copy(
+                src_ref=g_out.at[r],
+                dst_ref=g_in.at[r],
+                send_sem=pair_send.at[h],
+                recv_sem=pair_recv.at[h],
+                device_id={"dom": dom, "group": other},
+            )
+        )
+        pairs[-1].start()
+        pending.append(pairs[-1].wait_send)
+    g_own[...] = jnp.dot(x_t[core], dpre[...], preferred_element_type=F32)
+    for h in range(2):
+        pairs[h].wait_recv()
+        r = pl.ds(h * half, half)
+        summed = g_own[r, :] + g_in[r, :]
+        for k in range(PIECES // 2):
+            r, c = k // 2 * 16, k % 2 * TILE
+            part[h * PIECES // 2 + k] = summed[r : r + 16, c : c + TILE].astype(BF16)
 
     odd = lax.rem(my_x + my_y + core, 2)
     mine = my_y * (SIDE // 2) + lax.div(my_x, 2)
@@ -279,32 +283,35 @@
     def _():
         to_owner(*ODD[-1]).start()
 
+    store = pltpu.make_async_copy(out, out_any, out_sem)
+    store.start()
+    pending.append(store.wait)
+
     @pl.when(odd == 0)
     def _():
         pltpu.make_async_copy(part.at[mine], recv.at[dom], ph_recv.at[1]).start()
         wait_for(recv, ph_recv.at[1])
         z_part[...] = jnp.sum(recv[...].astype(F32), axis=0)
 
-        for i in Z_STEPS:
+        for g in along_z:
             pltpu.make_async_remote_copy(
                 src_ref=z_part,
                 dst_ref=recv_z.at[my_z],
                 send_sem=ph_send.at[2],
                 recv_sem=ph_recv.at[2],
-                device_id={"dom": dom, "group": lax.rem(my_z + i, SIDE) * 2 + core},
+                device_id={"dom": dom, "group": g},
             ).start()
         pltpu.make_async_copy(z_part, recv_z.at[my_z], ph_recv.at[2]).start()
         wait_for(recv_z, ph_recv.at[2])
         total[...] = (jnp.sum(recv_z[...], axis=0) * scale).astype(BF16)
 
-        for dx, dy in STEPS:
-            xi, yi = lax.rem(my_x + dx, SIDE), lax.rem(my_y + dy, SIDE)
+        for _, _, target in in_plane:
             pltpu.make_async_remote_copy(
                 src_ref=total,
                 dst_ref=gath.at[core, mine],
                 send_sem=ph_send.at[3],
                 recv_sem=ph_recv.at[3],
-                device_id={"dom": yi * SIDE + xi, "group": group},
+                device_id=target,
             ).start()
         pltpu.make_async_copy(total, gath.at[core, mine], ph_recv.at[3]).start()
 
@@ -380,8 +387,10 @@
             pltpu.VMEM((4, TILE, n_rows), BF16),
             pltpu.VMEM((4, TILE, width), BF16),
             pltpu.VMEM((2, width, n_rows), BF16),
-            pltpu.VMEM((SIDE, TILE, hid), F32),
+            pltpu.VMEM((n_rows, hid), F32),
+            pltpu.VMEM((n_rows, width), BF16),
             pltpu.VMEM((n_rows, hid), BF16),
+            pltpu.VMEM((width, hid), F32),
             pltpu.VMEM((width, hid), F32),
             pltpu.VMEM((width, hid), F32),
             pltpu.VMEM((PIECES, 16, TILE), BF16),
@@ -395,6 +404,8 @@
             pltpu.SemaphoreType.DMA,
             pltpu.SemaphoreType.DMA((4,)),
             pltpu.SemaphoreType.DMA((4,)),
+            pltpu.SemaphoreType.DMA((2,)),
+            pltpu.SemaphoreType.DMA((2,)),
             pltpu.SemaphoreType.DMA((5,)),
             pltpu.SemaphoreType.DMA((5,)),
         ],

time: 69.6 us -> 68.9 us (0.990)
  Pallas kernels: 68.8 us -> 68.1 us
    pallas_call x1, Pallas kernels: 67.9 us -> 67.1 us  [on_device(): pl.pallas_call(functools.partial(kernel, scale), out_shape=(pltpu.VMEM((n...]
where the time goes in v3:
time: 68.9 us; the launch traced here: 68.8 us
  Pallas kernels  68.1 us (99%)
    pallas_call x1, Pallas kernels, on_device(): pl.pallas_call(functools.partial(kernel, scale), out_shape=(pltpu.VMEM((n...  67.1 us

profile of v3, /device:TPU:1, one launch (start us, length us, event | category | flops | bytes accessed | tf_op | source)
XLA Modules:
  0.0 68.8 jit_solution(972085875942661190)
XLA Ops:
  0.6 67.1 %shard_map.112 = (bf16[1024,256]{1,0:T(8,128)(2,1)S(1)}, bf16[2,32,16,128]{3,2,1,0:T(8,128)(2,1)S(1)}) custom-call(bf16[512,256]{1,0:T(8,128)(2,1)} %bitcast.12, s32[1,64]{1,0:T(1,128)} %bitcast.15, s32[4,128]{1,0:T(4,128)} %bitcast.13, s32[1,4]{1,0:T(1,128)} %bitcast.16, s32[4,8]{1,0:T(4,128)} %bitcast.14, bf16[8,4,128,128]{3,2,1,0:T(8,128)(2,1)} %bitcast.10, ...), custom_call_target="tpu_custom_call" | custom-call | tf_op jit(solution)/shard_map/pallas_call | solution.py:366
  67.8 1.0 %shard_map.113 = (bf16[1024,256]{1,0:T(8,128)(2,1)}, f32[256,256]{1,0:T(8,128)}, f32[256,256]{1,0:T(8,128)}) custom-call(bf16[1024,256]{1,0:T(8,128)(2,1)S(1)} %get-tuple-element.8.out_in, bf16[2,32,16,128]{3,2,1,0:T(8,128)(2,1)S(1)} %get-tuple-element.9.gath), custom_call_target="tpu_custom_call" | custom-call | tf_op jit(solution)/shard_map/pallas_call | solution.py:431

commit v4 on v3

--- a/solution.py
+++ b/solution.py
@@ -15,6 +15,7 @@
 TILE = 128
 RB = 8
 PIECES = SIDE * SIDE // 2
+FAR_PIECE = SIDE // 2 * (SIDE // 2) + SIDE // 4
 Z_STEPS = (4, 3, 5, 2, 6, 1, 7)
 VMEM_LIMIT = 48 * 1024 * 1024
 
@@ -29,6 +30,24 @@
 )
 EVEN = [s for s in STEPS if sum(s) % 2 == 0] + [(0, 0)]
 ODD = [s for s in STEPS if sum(s) % 2 == 1]
+
+
+def homeward(fx, fy):
+    xs, ys = ([3, 4, 5, 6] if f else [7, 0, 1, 2] for f in (fx, fy))
+
+    def left(step):
+        return sum(ring((x + step[0]) % SIDE) for x in xs) + sum(
+            ring((y + step[1]) % SIDE) for y in ys
+        )
+
+    return sorted(STEPS, key=left)
+
+
+HOMEWARD = {(fx, fy): homeward(fx, fy) for fx in (0, 1) for fy in (0, 1)}
+
+
+def farthest(x, y):
+    return 1 - lax.div((x - 4) * (x - 4) + (y - 4) * (y - 4) + 31, 32)
 
 
 def iota(shape, axis):
@@ -98,6 +117,24 @@
     n_group = 2 * SIDE
     other = group + 1 - 2 * core
 
+    pairs_in = (
+        (owner_hbm, owner),
+        (feat_hbm, feat),
+        (rim_hbm, rim),
+        (cnt_hbm, cnt),
+        (src_hbm, src),
+        (ws_hbm, ws),
+        (wn_hbm, wn),
+        (val_hbm, val),
+        (cot_hbm, cot),
+    )
+    loads = [
+        pltpu.make_async_copy(a, b, in_sems.at[k]) for k, (a, b) in enumerate(pairs_in)
+    ]
+    l_owner, l_feat, l_rim, l_cnt, l_src, l_ws, l_wn, l_val, l_cot = loads
+    l_owner.start()
+    l_feat.start()
+
     barrier = pltpu.get_barrier_semaphore()
     group_next = lax.rem(group + 1, n_group)
     group_prev = lax.rem(group + n_group - 1, n_group)
@@ -110,28 +147,14 @@
         in_plane.append((xi, yi, {"dom": yi * SIDE + xi, "group": group}))
         pl.semaphore_signal(barrier, inc=1, device_id=in_plane[-1][2])
 
+    for load in loads[2:]:
+        load.start()
+
     pending = []
 
     def wait_for(like, sem):
         pltpu.make_async_copy(like, like, sem).wait()
 
-    loads = []
-    for k, (a, b) in enumerate(
-        (
-            (owner_hbm, owner),
-            (feat_hbm, feat),
-            (rim_hbm, rim),
-            (cnt_hbm, cnt),
-            (src_hbm, src),
-            (ws_hbm, ws),
-            (wn_hbm, wn),
-            (val_hbm, val),
-            (cot_hbm, cot),
-        )
-    ):
-        loads.append(pltpu.make_async_copy(a, b, in_sems.at[k]))
-        loads[-1].start()
-    l_owner, l_feat, l_rim, l_cnt, l_src, l_ws, l_wn, l_val, l_cot = loads
 
     blocks = owner.shape[1]
     rows = feat.shape[0]
@@ -264,20 +287,35 @@
             part[h * PIECES // 2 + k] = summed[r : r + 16, c : c + TILE].astype(BF16)
 
     odd = lax.rem(my_x + my_y + core, 2)
-    mine = my_y * (SIDE // 2) + lax.div(my_x, 2)
+    far = farthest(my_x, my_y) * (1 - core)
+    stand_in = 1 - lax.div((my_x - 1) * (my_x - 1) + my_y * my_y + core + 127, 128)
+    owns = (1 - odd) * (1 - far) + stand_in
+    mine = my_y * (SIDE // 2) + lax.div(my_x, 2) + stand_in * FAR_PIECE
 
     def to_owner(dx, dy):
         xi, yi = lax.rem(my_x + dx, SIDE), lax.rem(my_y + dy, SIDE)
+        moved = farthest(xi, yi) * (1 - core)
         return pltpu.make_async_remote_copy(
             src_ref=part.at[yi * (SIDE // 2) + lax.div(xi, 2)],
             dst_ref=recv.at[dom],
             send_sem=ph_send.at[1],
             recv_sem=ph_recv.at[1],
-            device_id={"dom": yi * SIDE + xi, "group": group},
+            device_id={
+                "dom": (yi - 4 * moved) * SIDE + xi - 3 * moved,
+                "group": group,
+            },
         )
 
     for (ex, ey), (ox, oy) in zip(EVEN[:-1], ODD[:-1]):
-        to_owner(ex + odd * (ox - ex), ey + odd * (oy - ey)).start()
+        copy = to_owner(ex + odd * (ox - ex), ey + odd * (oy - ey))
+        if (ox, oy) == (3, 4):
+            pl.when(stand_in == 0)(copy.start)
+        else:
+            copy.start()
+
+    @pl.when(far == 1)
+    def _():
+        to_owner(0, 0).start()
 
     @pl.when(odd == 1)
     def _():
@@ -287,7 +325,7 @@
     store.start()
     pending.append(store.wait)
 
-    @pl.when(odd == 0)
+    @pl.when(owns == 1)
     def _():
         pltpu.make_async_copy(part.at[mine], recv.at[dom], ph_recv.at[1]).start()
         wait_for(recv, ph_recv.at[1])
@@ -305,14 +343,22 @@
         wait_for(recv_z, ph_recv.at[2])
         total[...] = (jnp.sum(recv_z[...], axis=0) * scale).astype(BF16)
 
-        for _, _, target in in_plane:
-            pltpu.make_async_remote_copy(
-                src_ref=total,
-                dst_ref=gath.at[core, mine],
-                send_sem=ph_send.at[3],
-                recv_sem=ph_recv.at[3],
-                device_id=target,
-            ).start()
+        far_x = 1 - lax.div(lax.rem(my_x + 5, SIDE), 4)
+        far_y = 1 - lax.div(lax.rem(my_y + 5, SIDE), 4)
+
+        def to_plane(steps):
+            for dx, dy in steps:
+                xi, yi = lax.rem(my_x + dx, SIDE), lax.rem(my_y + dy, SIDE)
+                pltpu.make_async_remote_copy(
+                    src_ref=total,
+                    dst_ref=gath.at[core, mine],
+                    send_sem=ph_send.at[3],
+                    recv_sem=ph_recv.at[3],
+                    device_id={"dom": yi * SIDE + xi, "group": group},
+                ).start()
+
+        for (fx, fy), steps in HOMEWARD.items():
+            pl.when((far_x * 2 + far_y) == fx * 2 + fy)(functools.partial(to_plane, steps))
         pltpu.make_async_copy(total, gath.at[core, mine], ph_recv.at[3]).start()
 
     wait_for(gath.at[core], ph_recv.at[3])
@@ -325,11 +371,11 @@
     )
     back.start()
 
-    @pl.when(odd == 1)
+    @pl.when(owns == 0)
     def _():
         wait_for(recv.at[pl.ds(0, PIECES)], ph_send.at[1])
 
-    @pl.when(odd == 0)
+    @pl.when(owns == 1)
     def _():
         wait_for(recv.at[pl.ds(0, PIECES - 1)], ph_send.at[1])
         wait_for(recv_z.at[pl.ds(0, SIDE - 1)], ph_send.at[2])

time: 68.9 us -> 68.2 us (0.990)
  Pallas kernels: 68.1 us -> 67.4 us
    pallas_call x1, Pallas kernels: 67.1 us -> 66.4 us  [on_device(): pl.pallas_call(functools.partial(kernel, scale), out_shape=(pltpu.VMEM((n...]
where the time goes in v4:
time: 68.2 us; the launch traced here: 68 us
  Pallas kernels  67.4 us (99%)
    pallas_call x1, Pallas kernels, on_device(): pl.pallas_call(functools.partial(kernel, scale), out_shape=(pltpu.VMEM((n...  66.4 us

profile of v4, /device:TPU:1, one launch (start us, length us, event | category | flops | bytes accessed | tf_op | source)
XLA Modules:
  0.0 68.0 jit_solution(2064410708777280868)
XLA Ops:
  0.6 66.4 %shard_map.112 = (bf16[1024,256]{1,0:T(8,128)(2,1)S(1)}, bf16[2,32,16,128]{3,2,1,0:T(8,128)(2,1)S(1)}) custom-call(bf16[512,256]{1,0:T(8,128)(2,1)} %bitcast.12, s32[1,64]{1,0:T(1,128)} %bitcast.15, s32[4,128]{1,0:T(4,128)} %bitcast.13, s32[1,4]{1,0:T(1,128)} %bitcast.16, s32[4,8]{1,0:T(4,128)} %bitcast.14, bf16[8,4,128,128]{3,2,1,0:T(8,128)(2,1)} %bitcast.10, ...), custom_call_target="tpu_custom_call" | custom-call | tf_op jit(solution)/shard_map/pallas_call | solution.py:412
  67.0 1.0 %shard_map.113 = (bf16[1024,256]{1,0:T(8,128)(2,1)}, f32[256,256]{1,0:T(8,128)}, f32[256,256]{1,0:T(8,128)}) custom-call(bf16[1024,256]{1,0:T(8,128)(2,1)S(1)} %get-tuple-element.8.out_in, bf16[2,32,16,128]{3,2,1,0:T(8,128)(2,1)S(1)} %get-tuple-element.9.gath), custom_call_target="tpu_custom_call" | custom-call | tf_op jit(solution)/shard_map/pallas_call | solution.py:477

commit v5 on v4

--- a/solution.py
+++ b/solution.py
@@ -16,7 +16,8 @@
 RB = 8
 PIECES = SIDE * SIDE // 2
 FAR_PIECE = SIDE // 2 * (SIDE // 2) + SIDE // 4
-Z_STEPS = (4, 3, 5, 2, 6, 1, 7)
+Z_STEPS = (1, 2, 3, 4, 5, 6, 7)
+PARTS = 4
 VMEM_LIMIT = 48 * 1024 * 1024
 
 
@@ -261,10 +262,10 @@
         dpre[r, :] = (cot[r, :].astype(F32) * (sig + silu * (1.0 - sig))).astype(BF16)
 
     width = feat.shape[1]
-    half = width // 2
+    chunk = width // PARTS
     pairs = []
-    for h in range(2):
-        r = pl.ds(h * half, half)
+    for h in range(PARTS):
+        r = pl.ds(h * chunk, chunk)
         g_out[r, :] = jnp.dot(x_t[1 - core, r, :], dpre[...], preferred_element_type=F32)
         pairs.append(
             pltpu.make_async_remote_copy(
@@ -278,13 +279,13 @@
         pairs[-1].start()
         pending.append(pairs[-1].wait_send)
     g_own[...] = jnp.dot(x_t[core], dpre[...], preferred_element_type=F32)
-    for h in range(2):
+    for h in range(PARTS):
         pairs[h].wait_recv()
-        r = pl.ds(h * half, half)
+        r = pl.ds(h * chunk, chunk)
         summed = g_own[r, :] + g_in[r, :]
-        for k in range(PIECES // 2):
+        for k in range(PIECES // PARTS):
             r, c = k // 2 * 16, k % 2 * TILE
-            part[h * PIECES // 2 + k] = summed[r : r + 16, c : c + TILE].astype(BF16)
+            part[h * PIECES // PARTS + k] = summed[r : r + 16, c : c + TILE].astype(BF16)
 
     odd = lax.rem(my_x + my_y + core, 2)
     far = farthest(my_x, my_y) * (1 - core)
@@ -450,8 +451,8 @@
             pltpu.SemaphoreType.DMA,
             pltpu.SemaphoreType.DMA((4,)),
             pltpu.SemaphoreType.DMA((4,)),
-            pltpu.SemaphoreType.DMA((2,)),
-            pltpu.SemaphoreType.DMA((2,)),
+            pltpu.SemaphoreType.DMA((PARTS,)),
+            pltpu.SemaphoreType.DMA((PARTS,)),
             pltpu.SemaphoreType.DMA((5,)),
             pltpu.SemaphoreType.DMA((5,)),
         ],

time: 68.2 us -> 68.4 us (level)
  no operation moved by 1% of the time
where the time goes in v5:
time: 68.4 us; the launch traced here: 68.3 us
  Pallas kernels  67.6 us (99%)
    pallas_call x1, Pallas kernels, on_device(): pl.pallas_call(functools.partial(kernel, scale), out_shape=(pltpu.VMEM((n...  66.7 us

profile of v5, /device:TPU:1, one launch (start us, length us, event | category | flops | bytes accessed | tf_op | source)
XLA Modules:
  0.0 68.3 jit_solution(2675933418248300127)
XLA Ops:
  0.6 66.7 %shard_map.112 = (bf16[1024,256]{1,0:T(8,128)(2,1)S(1)}, bf16[2,32,16,128]{3,2,1,0:T(8,128)(2,1)S(1)}) custom-call(bf16[512,256]{1,0:T(8,128)(2,1)} %bitcast.12, s32[1,64]{1,0:T(1,128)} %bitcast.15, s32[4,128]{1,0:T(4,128)} %bitcast.13, s32[1,4]{1,0:T(1,128)} %bitcast.16, s32[4,8]{1,0:T(4,128)} %bitcast.14, bf16[8,4,128,128]{3,2,1,0:T(8,128)(2,1)} %bitcast.10, ...), custom_call_target="tpu_custom_call" | custom-call | tf_op jit(solution)/shard_map/pallas_call | solution.py:413
  67.3 1.0 %shard_map.113 = (bf16[1024,256]{1,0:T(8,128)(2,1)}, f32[256,256]{1,0:T(8,128)}, f32[256,256]{1,0:T(8,128)}) custom-call(bf16[1024,256]{1,0:T(8,128)(2,1)S(1)} %get-tuple-element.8.out_in, bf16[2,32,16,128]{3,2,1,0:T(8,128)(2,1)S(1)} %get-tuple-element.9.gath), custom_call_target="tpu_custom_call" | custom-call | tf_op jit(solution)/shard_map/pallas_call | solution.py:478
